TPU v7x, 512 devices: a whole 4x8x8 slice. The times are simulated.
512 devices in a mesh: batch: 128 (over x_hi, y, z), mp: 4 (over x_lo, core).
Axes of the slice: x: 4 (x_hi: 2, x_lo: 2; x = x_hi * 2 + x_lo), y: 8, z: 8, core: 2. Of those that a mesh axis runs over, the one named last changes fastest.
Arguments:
- queries: bfloat16 [1024, 4096], P('batch', 'mp')
- paraphrases: bfloat16 [1024, 4096], P('batch', 'mp')
- partner: int32 [1024], P('batch'), may hold values from 0 to 1023, as said below
- logit_scale: float32 [], replicated
Outputs:
- loss: float32 [], replicated
- grad_queries: bfloat16 [1024, 4096], P('batch', 'mp')
- grad_paraphrases: bfloat16 [1024, 4096], P('batch', 'mp')
Inputs may be any that keep to these rules, and one draw needn't show every extreme that they name: partner is a permutation of the 1024 paraphrase rows.
All inputs are finite; a program needn't handle non-finite values.
Results may differ from a plain program's by a relative error of at most 0.006.
Values may be sent and summed in bfloat16 or wider, within the bound.
A program may use at most 64 MiB of HBM per device.

v0:
```python
import jax
import jax.numpy as jnp
from jax import lax
from jax.sharding import PartitionSpec as P


def shards(queries, paraphrases, partner, logit_scale):
    rows = queries.shape[0]
    q_whole = queries.astype(jnp.float32)
    p_whole = paraphrases.astype(jnp.float32)
    q_sq, p_sq = lax.psum(
        (jnp.sum(q_whole * q_whole, axis=1), jnp.sum(p_whole * p_whole, axis=1)), "mp"
    )
    q_norm = jnp.sqrt(q_sq + 1e-06)
    p_norm = jnp.sqrt(p_sq + 1e-06)
    q_unit = q_whole / q_norm[:, None]
    p_unit = p_whole / p_norm[:, None]
    q_half = q_unit.astype(jnp.bfloat16)
    p_half = p_unit.astype(jnp.bfloat16)
    p_every = lax.all_gather(p_half, "batch", axis=0, tiled=True)
    total_rows = p_every.shape[0]
    partial_scores = lax.dot_general(
        q_half, p_every, (((1,), (1,)), ((), ())), preferred_element_type=jnp.float32
    )
    scores = logit_scale * lax.psum(partial_scores, "mp")
    row_max = jnp.max(scores, axis=1)
    row_lse = row_max + jnp.log(jnp.sum(jnp.exp(scores - row_max[:, None]), axis=1))
    local_max = jnp.max(scores, axis=0)
    col_max = lax.pmax(local_max, "batch")
    col_total = lax.psum(jnp.sum(jnp.exp(scores - col_max[None, :]), axis=0), "batch")
    col_lse = col_max + jnp.log(col_total)
    columns = lax.broadcasted_iota(jnp.int32, (rows, total_rows), 1)
    hit = (partner[:, None] == columns).astype(jnp.float32)
    positive = jnp.sum(hit * scores, axis=1)
    row_part = lax.psum(0.5 * jnp.sum(row_lse) - jnp.sum(positive), "batch")
    loss = row_part / total_rows + 0.5 * jnp.mean(col_lse)
    weights = (
        0.5 / total_rows * (jnp.exp(scores - row_lse[:, None]) + jnp.exp(scores - col_lse[None, :]))
        - hit / total_rows
    ).astype(jnp.bfloat16)
    d_q = logit_scale * jnp.dot(weights, p_every, preferred_element_type=jnp.float32)
    d_p = lax.psum_scatter(
        logit_scale
        * lax.dot_general(
            weights, q_half, (((0,), (0,)), ((), ())), preferred_element_type=jnp.float32
        ),
        "batch",
        scatter_dimension=0,
        tiled=True,
    )
    q_dot, p_dot = lax.psum((jnp.sum(q_unit * d_q, axis=1), jnp.sum(p_unit * d_p, axis=1)), "mp")
    grad_queries = ((d_q - q_unit * q_dot[:, None]) / q_norm[:, None]).astype(jnp.bfloat16)
    grad_paraphrases = ((d_p - p_unit * p_dot[:, None]) / p_norm[:, None]).astype(jnp.bfloat16)
    return (loss, grad_queries, grad_paraphrases)


def solution(mesh):
    return jax.shard_map(
        shards,
        mesh=mesh,
        in_specs=(P("batch", "mp"), P("batch", "mp"), P("batch"), P()),
        out_specs=(P(), P("batch", "mp"), P("batch", "mp")),
        check_vma=False,
    )
```

profile of v0, /device:TPU:1, one launch (start us, length us, event | category | flops | bytes accessed | tf_op | source)
XLA Modules:
  0.0 1614.4 jit_solution(17639950719372411106)
XLA Ops:
  7.2 0.0 copy-start.1
  7.2 0.0 copy-start.3
  7.2 0.0 all-gather.2.cloned.1.call-start
  7.2 0.9 fusion
  8.1 11.9 all-reduce.2
  20.0 1.4 fusion.5
  21.4 0.0 all-gather.2.cloned.1.call-update
  21.5 0.0 reduce-scatter.2.cloned.1.call-start
  22.2 124.2 %all-gather.2.cloned.1.call-done = bf16[1024,1024]{1,0:T(8,128)(2,1)} async-done(((bf16[8,1024]{1,0:T(8,128)(2,1)}), bf16[1024,1024]{1,0:T(8,128)(2,1)}) %all-gather.2.cloned.1.call-update) | async-done | bytes 2097168 | tf_op jit(solution)/shard_map/all_gather | solution.py:20
  146.3 2.2 fusion.3
  148.6 14.2 psum.51
  162.8 0.1 multiply_reduce_fusion.2
  162.9 299.9 %pmax.7 = f32[1024]{0:T(1024)S(1)} all-reduce(f32[1024]{0:T(1024)S(1)} %get-tuple-element.6), channel_id=1, replica_groups=mesh['batch'=128,'mp'=4] {'batch'}, use_global_device_ids=true, to_apply=%region_11.0 | all-reduce | flops 1024 | bytes 8192 | tf_op jit(solution)/shard_map/pmax | solution.py:29
  462.8 0.0 copy-done.3
  462.8 0.7 exponential_reduce_fusion
  463.5 0.6 fusion.7
  465.4 301.9 %all-reduce = (f32[]{:T(128)}, f32[1024]{0:T(1024)S(1)}) all-reduce(f32[]{:T(128)S(6)} %sub.46, f32[1024]{0:T(1024)S(1)} %get-tuple-element.3), channel_id=1, replica_groups=mesh['batch'=128,'mp'=4] {'batch'}, use_global_device_ids=true, to_apply=%region_9.0 | all-reduce | flops 1025 | bytes 8200 | tf_op jit(solution)/shard_map/psum | solution.py:35
  767.4 0.6 fusion.6
  768.0 0.0 copy-done.1
  768.0 2.8 convolution_multiply_fusion
  770.7 0.0 copy-start
  770.7 0.0 reduce-scatter.2.cloned.1.call-update
  770.7 0.0 copy-start.2
  772.2 0.1 copy-done
  772.3 0.5 multiply_reduce_fusion.1
  772.9 719.7 %reduce-scatter.2.cloned.1.call-done = f32[8,1024]{1,0:T(8,128)} async-done(((f32[1024,1024]{1,0:T(8,128)}), f32[8,1024]{1,0:T(8,128)}) %reduce-scatter.2.cloned.1.call-update) | async-done | bytes 32784 | tf_op jit(solution)/shard_map/reduce_scatter | solution.py:42
  1492.6 0.0 copy-done.2
  1492.6 0.9 multiply_reduce_fusion
  1493.5 110.8 %all-reduce.1 = (f32[8]{0:T(128)S(1)}, f32[8]{0:T(128)S(1)}) all-reduce(f32[8]{0:T(128)S(1)} %get-tuple-element.18, f32[8]{0:T(128)S(1)} %multiply_reduce_fusion), channel_id=1, replica_groups=mesh['batch'=128,'mp'=4] {'mp'}, use_global_device_ids=true, to_apply=%region_16.0 | all-reduce | flops 16 | bytes 128 | tf_op jit(solution)/shard_map/psum | solution.py:51
  1604.3 0.7 divide_convert_fusion.1
  1605.0 1.4 divide_convert_fusion
  (2 shorter events, 0.0 us)
Async XLA Ops:
  7.2 760.8 %copy-start.1 = (bf16[8,1024]{1,0:T(8,128)(2,1)S(1)}, bf16[8,1024]{1,0:T(8,128)(2,1)}, u32[]{:S(2)}) copy-start(bf16[8,1024]{1,0:T(8,128)(2,1)} %param.4) | copy-start | bytes 49156
  7.2 455.6 %copy-start.3 = (s32[8]{0:T(128)S(1)}, s32[8]{0:T(128)}, u32[]{:S(2)}) copy-start(s32[8]{0:T(128)} %param.6) | copy-start | bytes 100
  7.2 139.1 %all-gather.2.cloned.1.call-start = ((), (), s32[]{:S(2)}) async-start(), calls=%async_computation.1 | async-start | bytes 2113536 | tf_op jit(solution)/shard_map/all_gather | solution.py:20
  21.5 1471.1 %reduce-scatter.2.cloned.1.call-start = ((), (), s32[]{:S(2)}) async-start(), calls=%async_computation.2 | async-start | bytes 4227072 | tf_op jit(solution)/shard_map/reduce_scatter | solution.py:42
  770.7 1.6 copy-start
  770.7 721.8 %copy-start.2 = (bf16[8,1024]{1,0:T(8,128)(2,1)S(1)}, bf16[8,1024]{1,0:T(8,128)(2,1)}, u32[]{:S(2)}) copy-start(bf16[8,1024]{1,0:T(8,128)(2,1)} %param.5) | copy-start | bytes 49156
Sparse Core Ops, SparseCore 0:
  21.6 124.7 all-gather.1
  770.9 721.6 reduce-scatter.1
where the time goes:
time: 1610 us
  waiting for transfers between devices  844 us (52%)
  blocking collectives  739 us (46%)
  between operations  18.6 us (1%)
    reduce_scatter x1, waiting for transfers between devices, shards(): lax.psum_scatter(logit_scale * lax.dot_general(weights, q_half, (((0,), (...  720 us
    psum x1, blocking collectives, shards(): row_part = lax.psum(0.5 * jnp.sum(row_lse) - jnp.sum(positive), 'batch')  302 us
    pmax x1, blocking collectives, shards(): col_max = lax.pmax(local_max, 'batch')  300 us
    all_gather x1, waiting for transfers between devices, shards(): p_every = lax.all_gather(p_half, 'batch', axis=0, tiled=True)  124 us
    psum x1, blocking collectives, shards(): lax.psum((jnp.sum(q_unit * d_q, axis=1), jnp.sum(p_unit * d_p, axis=1)),...  111 us
  transfers between devices with their start and end apart: 2, of which 2 were waited for; matrix products, arithmetic and copies ran while one was open for 0% of the time, Pallas kernels for 0%

commit v1 on v0

v1 whole, which is shorter than its diff:
```python
import functools

import jax
import jax.numpy as jnp
from jax import lax
from jax.experimental import pallas as pl
from jax.experimental.pallas import tpu as pltpu
from jax.sharding import PartitionSpec as P

MESH = pl.DeviceIdType.MESH
F32 = jnp.float32
BF16 = jnp.bfloat16
GRID = (2, 8, 8)
NT = (((1,), (1,)), ((), ()))
NN = (((1,), (0,)), ((), ()))
OWN_Q, OWN_P, SWAP_Q, SWAP_P, FAR_Q, FAR_P, CORE, CHIP, ROWS, COLS, GRAD_Q, GRAD_P = range(12)


def dot(a, b, dims):
    return lax.dot_general(a, b, dims, preferred_element_type=F32)


def column(row):
    n = row.shape[1]
    return jnp.broadcast_to(row, (n, n)).T


def farthest_first(n):
    return sorted(range(1, n), key=lambda t: -min(t, n - t))


def kernel(grid, scale_ref, partner_any, q_any, p_any, loss_ref, gq_ref, gp_ref,
           partner_ref, q_in, p_in, qb, pb, qn, pn, part, part_core, half_sum, part_chip,
           row_stat, row_stats, col_stat, col_stats, gq, rq, gp, rp, load, send, recv):
    _, gy, gz = grid
    rows, feats = q_in.shape
    half = feats // 2
    nz, ny = gz * rows, gy * rows
    pairs = 2 * gy * nz
    b, m = lax.axis_index("batch"), lax.axis_index("mp")
    x, y, z = b // (gy * gz), b // gz % gy, b % gz

    z_peers = {t: (z + t) % gz for t in farthest_first(gz)}
    y_peers = {t: (y + t) % gy for t in farthest_first(gy)}
    z_peers = [(i, {"batch": (x * gy + y) * gz + i}) for i in z_peers.values()]
    y_peers = [(i, {"batch": (x * gy + i) * gz + z}) for i in y_peers.values()]
    x_peer = {"batch": ((1 - x) * gy + y) * gz + z}
    core_peer = {"mp": m // 2 * 2 + (m + 1) % 2}
    chip_peer = {"mp": (m + 2) % 4}

    barrier = pltpu.get_barrier_semaphore()
    everyone = [d for _, d in z_peers + y_peers] + [x_peer, chip_peer, core_peer]
    for d in everyone:
        pl.semaphore_signal(barrier, inc=1, device_id=d, device_id_type=MESH)
    loads = [
        pltpu.make_async_copy(source, target, load.at[i])
        for i, (source, target) in enumerate(
            ((q_any, q_in), (p_any, p_in), (partner_any, partner_ref))
        )
    ]
    for copy in loads:
        copy.start()

    def slot(ref, index, size=16):
        return ref.at[pl.ds(pl.multiple_of(index * size, size), size)]

    sent = []

    def push(src, dst, s, device):
        copy = pltpu.make_async_remote_copy(
            src_ref=src, dst_ref=dst, send_sem=send.at[s], recv_sem=recv.at[s],
            device_id=device, device_id_type=MESH,
        )
        copy.start()

    def arrived(ref, s, count, size):
        view = ref.at[pl.ds(0, count * size)]
        pltpu.make_async_copy(view, view, recv.at[s]).wait()
        sent.append((view, s))

    def halves(ref):
        whole = ref[...].astype(F32)
        return jnp.concatenate([whole[:, :half], whole[:, half:]], axis=0)

    for copy in loads:
        copy.wait()
    place = lax.broadcasted_iota(jnp.int32, (16, 128), 0)
    tag = jnp.zeros((16, 128), jnp.int32)
    for i in range(rows):
        tag = jnp.where(place == i, partner_ref[i] // 32, tag)
        tag = jnp.where(place == rows + i, partner_ref[i] % 32, tag)
    slot(qb, z)[...] = jnp.concatenate([halves(q_in), tag.astype(F32)], axis=1).astype(BF16)
    slot(pb, y)[...] = halves(p_in).astype(BF16)
    pl.semaphore_wait(barrier, len(everyone))

    push(slot(qb, z), slot(qb, gz + z), SWAP_Q, x_peer)
    push(slot(pb, y), slot(pb, gy + y), SWAP_P, x_peer)
    for t in range(max(gy, gz) - 1):
        if t < gz - 1:
            push(slot(qb, z), slot(qb, z), OWN_Q, z_peers[t][1])
        if t < gy - 1:
            push(slot(pb, y), slot(pb, y), OWN_P, y_peers[t][1])
    arrived(qb, SWAP_Q, 1, 16)
    arrived(pb, SWAP_P, 1, 16)
    for t in range(max(gy, gz) - 1):
        if t < gz - 1:
            push(slot(qb, gz + z), slot(qb, gz + z), FAR_Q, z_peers[t][1])
        if t < gy - 1:
            push(slot(pb, gy + y), slot(pb, gy + y), FAR_P, y_peers[t][1])

    def unpack(ref, out, r, n):
        whole = ref[r * n * 16:(r + 1) * n * 16, :half].astype(F32).reshape(n, 2, 8, half)
        whole = jnp.concatenate([whole[:, 0], whole[:, 1]], axis=2).reshape(n * 8, feats)
        out[r * n * 8:(r + 1) * n * 8, :] = whole.astype(BF16)
        square = whole * whole
        width = min(128, feats)
        return sum(square[:, c:c + width] for c in range(0, feats, width))

    arrived(qb, OWN_Q, gz - 1, 16)
    q_near = unpack(qb, qn, 0, gz)
    arrived(pb, OWN_P, gy - 1, 16)
    p_near = unpack(pb, pn, 0, gy)
    arrived(qb, FAR_Q, gz - 1, 16)
    q_far = unpack(qb, qn, 1, gz)
    arrived(pb, FAR_P, gy - 1, 16)
    p_far = unpack(pb, pn, 1, gy)

    q_sum = jnp.sum(jnp.concatenate([q_near, q_far], axis=0).T, axis=0, keepdims=True)
    p_sum = jnp.sum(jnp.concatenate([p_near, p_far], axis=0).T, axis=0, keepdims=True)
    part[0:2 * nz, :] = dot(qn[...], pn[...], NT)
    tile = lax.broadcasted_iota(jnp.int32, (8, 2 * ny), 0)
    part[2 * nz:2 * nz + 8, :] = jnp.where(tile == 0, q_sum, p_sum)
    size = 2 * nz + 8
    push(part, part_core, CORE, core_peer)
    arrived(part_core, CORE, 1, size)
    half_sum[...] = part[...] + part_core[...]
    push(half_sum, part_chip, CHIP, chip_peer)
    tags = qb[:, half:].astype(F32).reshape(2 * gz, 2, 8, 128)
    partner = (tags[:, 0] * 32.0 + tags[:, 1]).reshape(2 * nz, 128)[:, :2 * ny]
    lane = lax.broadcasted_iota(jnp.int32, (1, 2 * ny), 1)
    columns = (((x + lane // ny) % 2 * gy + lane // rows % gy) * gz + z) * rows + lane % rows
    hit = partner == columns.astype(F32)
    arrived(part_chip, CHIP, 1, size)
    total = half_sum[...] + part_chip[...]

    scale = scale_ref[0]
    q_inv = column(lax.rsqrt(total[2 * nz:2 * nz + 1] + 1e-6))
    p_inv = lax.rsqrt(total[2 * nz + 1:2 * nz + 2] + 1e-6)
    scores = (total[:2 * nz] * q_inv) * p_inv * scale
    across = scores.T

    def added(value, n):
        return jnp.sum(value[:n], axis=0, keepdims=True) + jnp.sum(value[n:], axis=0, keepdims=True)

    def both(row, n):
        return jnp.sum(row[:, :n]) + jnp.sum(row[:, n:])

    row_max = jnp.max(across, axis=0, keepdims=True)
    row_sum = added(jnp.exp(across - row_max), ny)
    col_max = jnp.max(scores, axis=0, keepdims=True)
    col_sum = added(jnp.exp(scores - col_max), nz)
    held = jnp.where(hit, scores, 0.0)
    near, far = (jnp.sum(held[r:r + nz], axis=0, keepdims=True) for r in (0, nz))
    hits = (jnp.sum(near[:, :ny]) + jnp.sum(far[:, ny:])) + (jnp.sum(near[:, ny:]) + jnp.sum(far[:, :ny]))
    stat = lax.broadcasted_iota(jnp.int32, (8, 2 * nz), 0)
    row_stat[...] = jnp.where(stat == 0, row_max, jnp.where(stat == 1, row_sum, hits))
    stat = lax.broadcasted_iota(jnp.int32, (8, 2 * ny), 0)
    col_stat[...] = jnp.where(stat == 0, col_max, col_sum)
    for t in range(max(gy, gz) - 1):
        if t < gz - 1:
            push(row_stat, slot(row_stats, z, 8), ROWS, z_peers[t][1])
        if t < gy - 1:
            push(col_stat, slot(col_stats, y, 8), COLS, y_peers[t][1])
    slot(row_stats, z, 8)[...] = row_stat[...]
    slot(col_stats, y, 8)[...] = col_stat[...]
    p_inv_col = column(p_inv)[:ny, :1]
    q_inv_col = q_inv[:nz, :1]

    def lse(ref, n):
        stats = ref[...].reshape(n, 8, ref.shape[1])
        most = jnp.max(stats[:, 0:1], axis=0)
        summed = jnp.sum(stats[:, 1:2] * jnp.exp(stats[:, 0:1] - most), axis=0)
        return most + jnp.log(summed), stats

    arrived(row_stats, ROWS, gz - 1, 8)
    row_lse, stats = lse(row_stats, gz)
    row_lse_col = column(row_lse)
    arrived(col_stats, COLS, gy - 1, 8)
    col_lse, _ = lse(col_stats, gy)

    weights = 0.5 / pairs * (jnp.exp(scores - row_lse_col) + jnp.exp(scores - col_lse))
    weights = weights - jnp.where(hit, 1.0 / pairs, 0.0)
    weights = weights.astype(BF16).astype(F32)
    turned = weights.T[:ny]
    weights = weights[:nz]

    def share(weight, score, other_inv, other, mine, mine_inv):
        n = weight.shape[0]
        scaled = weight * (scale * other_inv)
        high = scaled.astype(BF16).astype(F32)
        twice = jnp.concatenate([high, scaled - high], axis=0).astype(BF16)
        d = dot(twice, other, NN)
        along = jnp.sum(weight * score, axis=1, keepdims=True)
        d = (d[:n] + d[n:] - mine.astype(F32) * (along * mine_inv)) * mine_inv
        d = d.reshape(n // 8, 8, feats)
        return jnp.concatenate([d[:, :, :half], d[:, :, half:]], axis=1).reshape(n * 2, half)

    def extra(value, n):
        high = value.astype(BF16).astype(F32)
        middle = (value - high).astype(BF16).astype(F32)
        low = value - high - middle
        ext = jnp.where(place == 0, high, 0.0)
        ext = jnp.where(place == 1, middle, ext)
        ext = jnp.where(place == 2, low, ext).astype(BF16)
        return jnp.broadcast_to(ext[None], (n, 16, 128)).reshape(n * 16, 128)

    positives = jnp.sum(stats[:, 2:3, 0:1])
    gq[:, :half] = share(weights, scores[:nz], p_inv, pn[...], qn[0:nz, :], q_inv_col).astype(BF16)
    gq[:, half:] = extra(jnp.full((16, 128), 0.5 * both(col_lse, ny)), gz)
    for i, device in z_peers:
        push(slot(gq, i), slot(rq, z), GRAD_Q, device)
    slot(rq, z)[...] = slot(gq, z)[...]
    q_inv_row = lax.rsqrt(total[2 * nz:2 * nz + 1] + 1e-6)
    gp[:, :half] = share(turned, across[:ny], q_inv_row, qn[...], pn[0:ny, :], p_inv_col).astype(BF16)
    gp[:, half:] = extra(jnp.full((16, 128), 0.5 * both(row_lse, nz) - positives), gy)
    for i, device in y_peers:
        push(slot(gp, i), slot(rp, y), GRAD_P, device)
    slot(rp, y)[...] = slot(gp, y)[...]

    def gathered(ref, n, out_ref):
        whole = jnp.sum(ref[...].astype(F32).reshape(n, 16, half + 128), axis=0)
        out_ref[...] = jnp.concatenate([whole[:8, :half], whole[8:, :half]], axis=1).astype(BF16)
        return jnp.sum(whole[:, half:half + 1])

    arrived(rq, GRAD_Q, gz - 1, 16)
    loss = gathered(rq, gz, gq_ref)
    arrived(rp, GRAD_P, gy - 1, 16)
    loss_ref[0] = (loss + gathered(rp, gy, gp_ref)) / pairs
    for view, s in sent:
        pltpu.make_async_copy(view, view, send.at[s]).wait()


def build(mesh, grid):
    _, gy, gz = grid

    def shards(queries, paraphrases, partner, logit_scale):
        rows, feats = queries.shape
        half = feats // 2
        nz, ny = gz * rows, gy * rows
        vmem, smem = pl.BlockSpec(memory_space=pltpu.VMEM), pl.BlockSpec(memory_space=pltpu.SMEM)
        anywhere = pl.BlockSpec(memory_space=pl.ANY)
        block = pltpu.VMEM((2 * nz + 8, 2 * ny), F32)
        loss, grad_q, grad_p = pl.pallas_call(
            functools.partial(kernel, grid),
            out_shape=(
                jax.ShapeDtypeStruct((1,), F32),
                jax.ShapeDtypeStruct((rows, feats), BF16),
                jax.ShapeDtypeStruct((rows, feats), BF16),
            ),
            in_specs=[smem, anywhere, anywhere, anywhere],
            out_specs=(smem, vmem, vmem),
            scratch_shapes=[
                pltpu.SMEM((rows,), jnp.int32),
                pltpu.VMEM((rows, feats), BF16),
                pltpu.VMEM((rows, feats), BF16),
                pltpu.VMEM((gz * 32, half + 128), BF16),
                pltpu.VMEM((gy * 32, half), BF16),
                pltpu.VMEM((2 * nz, feats), BF16),
                pltpu.VMEM((2 * ny, feats), BF16),
                block,
                block,
                block,
                block,
                pltpu.VMEM((8, 2 * nz), F32),
                pltpu.VMEM((gz * 8, 2 * nz), F32),
                pltpu.VMEM((8, 2 * ny), F32),
                pltpu.VMEM((gy * 8, 2 * ny), F32),
                pltpu.VMEM((gz * 16, half + 128), BF16),
                pltpu.VMEM((gz * 16, half + 128), BF16),
                pltpu.VMEM((gy * 16, half + 128), BF16),
                pltpu.VMEM((gy * 16, half + 128), BF16),
                pltpu.SemaphoreType.DMA((3,)),
                pltpu.SemaphoreType.DMA((12,)),
                pltpu.SemaphoreType.DMA((12,)),
            ],
            compiler_params=pltpu.CompilerParams(
                collective_id=0, has_side_effects=True, vmem_limit_bytes=32 * 1024 * 1024
            ),
        )(logit_scale.reshape(1), partner, queries, paraphrases)
        return loss[0], grad_q, grad_p

    if mesh is None:
        return shards
    return jax.shard_map(
        shards,
        mesh=mesh,
        in_specs=(P("batch", "mp"), P("batch", "mp"), P("batch"), P()),
        out_specs=(P(), P("batch", "mp"), P("batch", "mp")),
        check_vma=False,
    )


def solution(mesh):
    return build(mesh, GRID)
```

time: 1610 us -> 46.3 us (0.03)
  waiting for transfers between devices: 844 us -> 0 us
  blocking collectives: 739 us -> 0 us
  Pallas kernels: 0 us -> 39.2 us
    reduce_scatter x1 -> x0, waiting for transfers between devices: 720 us -> none  [shards(): lax.psum_scatter(logit_scale * lax.dot_general(weights, q_half, (((0,), (...]
    psum x4 -> x0, blocking collectives: 439 us -> none  [the longest x1 302 us: shards(): row_part = lax.psum(0.5 * jnp.sum(row_lse) - jnp.sum(positive), 'batch')]
    pmax x1 -> x0, blocking collectives: 300 us -> none  [shards(): col_max = lax.pmax(local_max, 'batch')]
    all_gather x1 -> x0, waiting for transfers between devices: 124 us -> none  [shards(): p_every = lax.all_gather(p_half, 'batch', axis=0, tiled=True)]
    pallas_call x0 -> x1, Pallas kernels: none -> 39.2 us  [shards(): pl.pallas_call(functools.partial(kernel, grid), out_shape=(jax.ShapeDtype...]
  transfers between devices with their start and end apart: 2 -> 0, of which waited for: 2 -> 0; matrix products, arithmetic and copies ran while one was open for 0% -> 0% of each run, Pallas kernels for 0% -> 0%
where the time goes in v1:
time: 46.3 us; the launch traced here: 45.6 us
  Pallas kernels  39.2 us (85%)
  local copies, waits for them, and re-layouts  3.29 us (7%)
  between operations  3.03 us (7%)
    pallas_call x1, Pallas kernels, shards(): pl.pallas_call(functools.partial(kernel, grid), out_shape=(jax.ShapeDtype...  39.2 us
    unnamed x8, local copies, waits for them, and re-layouts  3.29 us

profile of v1, /device:TPU:1, one launch (start us, length us, event | category | flops | bytes accessed | tf_op | source)
XLA Modules:
  0.0 45.6 jit_solution(10847993936384008505)
XLA Ops:
  1.3 0.0 copy-start.2
  1.3 0.6 %copy-done.2 = s32[8]{0:T(128)S(1)} copy-done((s32[8]{0:T(128)S(1)}, s32[8]{0:T(128)}, u32[]{:S(2)}) %copy-start.2) | copy-done | bytes 56
  1.9 0.0 copy-start
  1.9 0.7 %copy-done = bf16[8,1024]{1,0:T(8,128)(2,1)S(1)} copy-done((bf16[8,1024]{1,0:T(8,128)(2,1)S(1)}, bf16[8,1024]{1,0:T(8,128)(2,1)}, u32[]{:S(2)}) %copy-start) | copy-done | bytes 16408
  2.7 0.0 copy-start.1
  2.7 0.7 %copy-done.1 = bf16[8,1024]{1,0:T(8,128)(2,1)S(1)} copy-done((bf16[8,1024]{1,0:T(8,128)(2,1)S(1)}, bf16[8,1024]{1,0:T(8,128)(2,1)}, u32[]{:S(2)}) %copy-start.1) | copy-done | bytes 16408
  3.4 39.2 %shard_map.67 = (f32[1]{0:T(128)}, bf16[8,1024]{1,0:T(8,128)(2,1)S(1)}, bf16[8,1024]{1,0:T(8,128)(2,1)S(1)}) custom-call(f32[1]{0:T(128)} %bitcast.2.scale_ref, s32[8]{0:T(128)S(1)} %copy-done.2, bf16[8,1024]{1,0:T(8,128)(2,1)S(1)} %copy-done, bf16[8,1024]{1,0:T(8,128)(2,1)S(1)} %copy-done.1), custom_call_target="tpu_custom_call" | custom-call | tf_op jit(solution)/shard_map/pallas_call | solution.py:253
  43.2 0.6 %copy.12 = bf16[8,1024]{1,0:T(8,128)(2,1)} copy(bf16[8,1024]{1,0:T(8,128)(2,1)S(1)} %get-tuple-element.13) | data formatting | bytes 32768
  43.8 0.6 %copy.13 = bf16[8,1024]{1,0:T(8,128)(2,1)} copy(bf16[8,1024]{1,0:T(8,128)(2,1)S(1)} %get-tuple-element.14) | data formatting | bytes 32768
Async XLA Ops:
  1.3 0.7 %copy-start.2 = (s32[8]{0:T(128)S(1)}, s32[8]{0:T(128)}, u32[]{:S(2)}) copy-start(s32[8]{0:T(128)} %partner_any.1) | copy-start | bytes 100
  1.9 0.7 %copy-start = (bf16[8,1024]{1,0:T(8,128)(2,1)S(1)}, bf16[8,1024]{1,0:T(8,128)(2,1)}, u32[]{:S(2)}) copy-start(bf16[8,1024]{1,0:T(8,128)(2,1)} %q_any.1) | copy-start | bytes 49156
  2.7 0.7 %copy-start.1 = (bf16[8,1024]{1,0:T(8,128)(2,1)S(1)}, bf16[8,1024]{1,0:T(8,128)(2,1)}, u32[]{:S(2)}) copy-start(bf16[8,1024]{1,0:T(8,128)(2,1)} %p_any.1) | copy-start | bytes 49156

commit v2 on v1

--- a/solution.py
+++ b/solution.py
@@ -13,7 +13,7 @@
 GRID = (2, 8, 8)
 NT = (((1,), (1,)), ((), ()))
 NN = (((1,), (0,)), ((), ()))
-OWN_Q, OWN_P, SWAP_Q, SWAP_P, FAR_Q, FAR_P, CORE, CHIP, ROWS, COLS, GRAD_Q, GRAD_P = range(12)
+OWN_Q, OWN_P, SWAP_Q, SWAP_P, FAR_Q, FAR_P, CORE, LEFT, RIGHT, ROWS, COLS, GRAD_Q, GRAD_P = range(13)
 
 
 def dot(a, b, dims):
@@ -29,9 +29,9 @@
     return sorted(range(1, n), key=lambda t: -min(t, n - t))
 
 
-def kernel(grid, scale_ref, partner_any, q_any, p_any, loss_ref, gq_ref, gp_ref,
-           partner_ref, q_in, p_in, qb, pb, qn, pn, part, part_core, half_sum, part_chip,
-           row_stat, row_stats, col_stat, col_stats, gq, rq, gp, rp, load, send, recv):
+def kernel(grid, scale_any, partner_any, q_any, p_any, rq, rp,
+           scale_ref, partner_ref, q_in, p_in, qb, pb, qn, pn, part, part_core, part_left, part_right,
+           row_stat, row_stats, col_stat, col_stats, gq, gp, load, send, recv):
     _, gy, gz = grid
     rows, feats = q_in.shape
     half = feats // 2
@@ -45,17 +45,19 @@
     z_peers = [(i, {"batch": (x * gy + y) * gz + i}) for i in z_peers.values()]
     y_peers = [(i, {"batch": (x * gy + i) * gz + z}) for i in y_peers.values()]
     x_peer = {"batch": ((1 - x) * gy + y) * gz + z}
+    core, other = m % 2, (m + 2) % 4 // 2 * 2
     core_peer = {"mp": m // 2 * 2 + (m + 1) % 2}
-    chip_peer = {"mp": (m + 2) % 4}
+    left_peers = [{"mp": other + c} for c in range(2)]
+    right_peers = [{"batch": x_peer["batch"], "mp": other + c} for c in range(2)]
 
     barrier = pltpu.get_barrier_semaphore()
-    everyone = [d for _, d in z_peers + y_peers] + [x_peer, chip_peer, core_peer]
+    everyone = [d for _, d in z_peers + y_peers] + [x_peer, *left_peers, *right_peers, core_peer]
     for d in everyone:
         pl.semaphore_signal(barrier, inc=1, device_id=d, device_id_type=MESH)
     loads = [
         pltpu.make_async_copy(source, target, load.at[i])
         for i, (source, target) in enumerate(
-            ((q_any, q_in), (p_any, p_in), (partner_any, partner_ref))
+            ((q_any, q_in), (p_any, p_in), (partner_any, partner_ref), (scale_any, scale_ref))
         )
     ]
     for copy in loads:
@@ -127,26 +129,34 @@
 
     q_sum = jnp.sum(jnp.concatenate([q_near, q_far], axis=0).T, axis=0, keepdims=True)
     p_sum = jnp.sum(jnp.concatenate([p_near, p_far], axis=0).T, axis=0, keepdims=True)
-    part[0:2 * nz, :] = dot(qn[...], pn[...], NT)
+    part[0:nz, :] = dot(qn[nz:, :], pn[...], NT)
+    part[nz:2 * nz, :] = dot(qn[0:nz, :], pn[...], NT)
     tile = lax.broadcasted_iota(jnp.int32, (8, 2 * ny), 0)
     part[2 * nz:2 * nz + 8, :] = jnp.where(tile == 0, q_sum, p_sum)
     size = 2 * nz + 8
+    for device in left_peers:
+        push(part.at[pl.ds(nz, nz + 8)], slot(part_left, core, nz + 8), LEFT, device)
+    for device in right_peers:
+        push(part.at[pl.ds(nz, nz)], slot(part_right, core, nz), RIGHT, device)
     push(part, part_core, CORE, core_peer)
-    arrived(part_core, CORE, 1, size)
-    half_sum[...] = part[...] + part_core[...]
-    push(half_sum, part_chip, CHIP, chip_peer)
     tags = qb[:, half:].astype(F32).reshape(2 * gz, 2, 8, 128)
     partner = (tags[:, 0] * 32.0 + tags[:, 1]).reshape(2 * nz, 128)[:, :2 * ny]
     lane = lax.broadcasted_iota(jnp.int32, (1, 2 * ny), 1)
     columns = (((x + lane // ny) % 2 * gy + lane // rows % gy) * gz + z) * rows + lane % rows
     hit = partner == columns.astype(F32)
-    arrived(part_chip, CHIP, 1, size)
-    total = half_sum[...] + part_chip[...]
+    arrived(part_core, CORE, 1, size)
+    total = part[...] + part_core[...]
+    arrived(part_left, LEFT, 2, nz + 8)
+    left = part_left[0:nz + 8, :] + part_left[nz + 8:, :]
+    arrived(part_right, RIGHT, 2, nz)
+    right = pltpu.roll(part_right[0:nz, :] + part_right[nz:, :], ny, 1)
+    total = total + jnp.concatenate([right, left], axis=0)
 
     scale = scale_ref[0]
     q_inv = column(lax.rsqrt(total[2 * nz:2 * nz + 1] + 1e-6))
     p_inv = lax.rsqrt(total[2 * nz + 1:2 * nz + 2] + 1e-6)
-    scores = (total[:2 * nz] * q_inv) * p_inv * scale
+    product = jnp.concatenate([total[nz:2 * nz], total[:nz]], axis=0)
+    scores = (product * q_inv) * p_inv * scale
     across = scores.T
 
     def added(value, n):
@@ -219,25 +229,33 @@
     gq[:, half:] = extra(jnp.full((16, 128), 0.5 * both(col_lse, ny)), gz)
     for i, device in z_peers:
         push(slot(gq, i), slot(rq, z), GRAD_Q, device)
-    slot(rq, z)[...] = slot(gq, z)[...]
+    keep_q = pltpu.make_async_copy(slot(gq, z), slot(rq, z), load.at[0])
+    keep_q.start()
     q_inv_row = lax.rsqrt(total[2 * nz:2 * nz + 1] + 1e-6)
     gp[:, :half] = share(turned, across[:ny], q_inv_row, qn[...], pn[0:ny, :], p_inv_col).astype(BF16)
     gp[:, half:] = extra(jnp.full((16, 128), 0.5 * both(row_lse, nz) - positives), gy)
     for i, device in y_peers:
         push(slot(gp, i), slot(rp, y), GRAD_P, device)
-    slot(rp, y)[...] = slot(gp, y)[...]
-
-    def gathered(ref, n, out_ref):
-        whole = jnp.sum(ref[...].astype(F32).reshape(n, 16, half + 128), axis=0)
+    keep_p = pltpu.make_async_copy(slot(gp, y), slot(rp, y), load.at[1])
+    keep_p.start()
+
+    keep_q.wait()
+    keep_p.wait()
+    arrived(rq, GRAD_Q, gz - 1, 16)
+    arrived(rp, GRAD_P, gy - 1, 16)
+    for view, s in sent:
+        pltpu.make_async_copy(view, view, send.at[s]).wait()
+
+
+def finish(pairs, rq, rp, loss_ref, gq_ref, gp_ref):
+    half = gq_ref.shape[1] // 2
+
+    def gathered(ref, out_ref):
+        whole = jnp.sum(ref[...].astype(F32).reshape(-1, 16, half + 128), axis=0)
         out_ref[...] = jnp.concatenate([whole[:8, :half], whole[8:, :half]], axis=1).astype(BF16)
         return jnp.sum(whole[:, half:half + 1])
 
-    arrived(rq, GRAD_Q, gz - 1, 16)
-    loss = gathered(rq, gz, gq_ref)
-    arrived(rp, GRAD_P, gy - 1, 16)
-    loss_ref[0] = (loss + gathered(rp, gy, gp_ref)) / pairs
-    for view, s in sent:
-        pltpu.make_async_copy(view, view, send.at[s]).wait()
+    loss_ref[0] = (gathered(rq, gq_ref) + gathered(rp, gp_ref)) / pairs
 
 
 def build(mesh, grid):
@@ -250,16 +268,16 @@
         vmem, smem = pl.BlockSpec(memory_space=pltpu.VMEM), pl.BlockSpec(memory_space=pltpu.SMEM)
         anywhere = pl.BlockSpec(memory_space=pl.ANY)
         block = pltpu.VMEM((2 * nz + 8, 2 * ny), F32)
-        loss, grad_q, grad_p = pl.pallas_call(
+        shares_q, shares_p = pl.pallas_call(
             functools.partial(kernel, grid),
             out_shape=(
-                jax.ShapeDtypeStruct((1,), F32),
-                jax.ShapeDtypeStruct((rows, feats), BF16),
-                jax.ShapeDtypeStruct((rows, feats), BF16),
+                jax.ShapeDtypeStruct((gz * 16, half + 128), BF16),
+                jax.ShapeDtypeStruct((gy * 16, half + 128), BF16),
             ),
-            in_specs=[smem, anywhere, anywhere, anywhere],
-            out_specs=(smem, vmem, vmem),
+            in_specs=[anywhere] * 4,
+            out_specs=(anywhere, anywhere),
             scratch_shapes=[
+                pltpu.SMEM((1,), F32),
                 pltpu.SMEM((rows,), jnp.int32),
                 pltpu.VMEM((rows, feats), BF16),
                 pltpu.VMEM((rows, feats), BF16),
@@ -269,24 +287,33 @@
                 pltpu.VMEM((2 * ny, feats), BF16),
                 block,
                 block,
-                block,
-                block,
+                pltpu.VMEM((2 * (nz + 8), 2 * ny), F32),
+                pltpu.VMEM((2 * nz, 2 * ny), F32),
                 pltpu.VMEM((8, 2 * nz), F32),
                 pltpu.VMEM((gz * 8, 2 * nz), F32),
                 pltpu.VMEM((8, 2 * ny), F32),
                 pltpu.VMEM((gy * 8, 2 * ny), F32),
                 pltpu.VMEM((gz * 16, half + 128), BF16),
-                pltpu.VMEM((gz * 16, half + 128), BF16),
                 pltpu.VMEM((gy * 16, half + 128), BF16),
-                pltpu.VMEM((gy * 16, half + 128), BF16),
-                pltpu.SemaphoreType.DMA((3,)),
-                pltpu.SemaphoreType.DMA((12,)),
-                pltpu.SemaphoreType.DMA((12,)),
+                pltpu.SemaphoreType.DMA((4,)),
+                pltpu.SemaphoreType.DMA((13,)),
+                pltpu.SemaphoreType.DMA((13,)),
             ],
             compiler_params=pltpu.CompilerParams(
-                collective_id=0, has_side_effects=True, vmem_limit_bytes=32 * 1024 * 1024
+                collective_id=0, has_side_effects=True, vmem_limit_bytes=60 * 1024 * 1024
             ),
         )(logit_scale.reshape(1), partner, queries, paraphrases)
+        loss, grad_q, grad_p = pl.pallas_call(
+            functools.partial(finish, 2 * gy * nz),
+            out_shape=(
+                jax.ShapeDtypeStruct((1,), F32),
+                jax.ShapeDtypeStruct((rows, feats), BF16),
+                jax.ShapeDtypeStruct((rows, feats), BF16),
+            ),
+            in_specs=[vmem, vmem],
+            out_specs=(smem, vmem, vmem),
+            compiler_params=pltpu.CompilerParams(vmem_limit_bytes=60 * 1024 * 1024),
+        )(shares_q, shares_p)
         return loss[0], grad_q, grad_p
 
     if mesh is None:

time: 46.3 us -> 42.1 us (0.909); the launches traced: 45.6 us -> 41.9 us
  local copies, waits for them, and re-layouts: 3.29 us -> 0 us
  between operations: 3.03 us -> 1.29 us
  Pallas kernels: 39.2 us -> 40.6 us
    unnamed x8 -> x0, local copies, waits for them, and re-layouts: 3.29 us -> none
    pallas_call x0 -> x1, Pallas kernels: none -> 1.65 us  [shards(): pl.pallas_call(functools.partial(finish, 2 * gy * nz), out_shape=(jax.Sha...]
where the time goes in v2:
time: 42.1 us; the launch traced here: 41.9 us
  Pallas kernels  40.6 us (96%)
  between operations  1.29 us (3%)
    pallas_call x1, Pallas kernels, shards(): pl.pallas_call(functools.partial(kernel, grid), out_shape=(jax.ShapeDtype...  38.9 us
    pallas_call x1, Pallas kernels, shards(): pl.pallas_call(functools.partial(finish, 2 * gy * nz), out_shape=(jax.Sha...  1.65 us

profile of v2, /device:TPU:1, one launch (start us, length us, event | category | flops | bytes accessed | tf_op | source)
XLA Modules:
  0.0 41.9 jit_solution(11592159003158668494)
XLA Ops:
  1.3 38.9 %shard_map.67 = (bf16[128,640]{1,0:T(8,128)(2,1)}, bf16[128,640]{1,0:T(8,128)(2,1)}) custom-call(f32[1]{0:T(128)} %bitcast.2.scale_any, s32[8]{0:T(128)} %partner_any.1, bf16[8,1024]{1,0:T(8,128)(2,1)} %q_any.1, bf16[8,1024]{1,0:T(8,128)(2,1)} %p_any.1), custom_call_target="tpu_custom_call" | custom-call | tf_op jit(solution)/shard_map/pallas_call | solution.py:271
  40.2 1.7 %shard_map.68 = (f32[1]{0:T(128)}, bf16[8,1024]{1,0:T(8,128)(2,1)}, bf16[8,1024]{1,0:T(8,128)(2,1)}) custom-call(bf16[128,640]{1,0:T(8,128)(2,1)} %get-tuple-element.8.rq, bf16[128,640]{1,0:T(8,128)(2,1)} %get-tuple-element.9.rp), custom_call_target="tpu_custom_call" | custom-call | tf_op jit(solution)/shard_map/pallas_call | solution.py:306

commit v3 on v2

v3 whole, which is shorter than its diff:
```python
import functools

import jax
import jax.numpy as jnp
from jax import lax
from jax.experimental import pallas as pl
from jax.experimental.pallas import tpu as pltpu
from jax.sharding import PartitionSpec as P

MESH = pl.DeviceIdType.MESH
F32 = jnp.float32
BF16 = jnp.bfloat16
GRID = (2, 8, 8)
NT = (((1,), (1,)), ((), ()))
NN = (((1,), (0,)), ((), ()))
OWN_Q, OWN_P, SWAP_Q, SWAP_P, FAR_Q, FAR_P, CORE, LEFT, RIGHT, ROWS, COLS, GRAD_Q, GRAD_P, OWN_T, SWAP_T, FAR_T,\
    CORE_E, LEFT_E, RIGHT_E, LOSS_Z, LOSS_Y = range(21)


def dot(a, b, dims):
    return lax.dot_general(a, b, dims, preferred_element_type=F32)


def column(row):
    n = row.shape[1]
    return jnp.broadcast_to(row, (n, n)).T


def farthest_first(n):
    return sorted(range(1, n), key=lambda t: -min(t, n - t))


def kernel(grid, scale_any, partner_any, q_any, p_any, rq, rp, loss_z, loss_y,
           scale_ref, partner_ref, q_in, p_in, qb, pb, qn, pn, part, part_core, part_left, part_right,
           first, first_core, first_left, first_right,
           row_stat, row_stats, col_stat, col_stats, gq, gp, tags, q_less, p_less, loss_part, load, send, recv):
    _, gy, gz = grid
    rows, feats = q_in.shape
    half = feats // 2
    nz, ny = gz * rows, gy * rows
    pairs = 2 * gy * nz
    b, m = lax.axis_index("batch"), lax.axis_index("mp")
    x, y, z = b // (gy * gz), b // gz % gy, b % gz

    z_peers = {t: (z + t) % gz for t in farthest_first(gz)}
    y_peers = {t: (y + t) % gy for t in farthest_first(gy)}
    z_peers = [(i, {"batch": (x * gy + y) * gz + i}) for i in z_peers.values()]
    y_peers = [(i, {"batch": (x * gy + i) * gz + z}) for i in y_peers.values()]
    x_peer = {"batch": ((1 - x) * gy + y) * gz + z}
    core, other = m % 2, (m + 2) % 4 // 2 * 2
    core_peer = {"mp": m // 2 * 2 + (m + 1) % 2}
    left_peers = [{"mp": other + c} for c in range(2)]
    right_peers = [{"batch": x_peer["batch"], "mp": other + c} for c in range(2)]

    loads = [
        pltpu.make_async_copy(source, target, load.at[i])
        for i, (source, target) in enumerate(
            ((q_any, q_in), (p_any, p_in), (partner_any, partner_ref), (scale_any, scale_ref))
        )
    ]
    for copy in loads:
        copy.start()
    barrier = pltpu.get_barrier_semaphore()
    everyone = [x_peer] + [d for pair in zip(z_peers, y_peers) for _, d in pair] + [*left_peers, *right_peers, core_peer]
    for d in everyone:
        pl.semaphore_signal(barrier, inc=1, device_id=d, device_id_type=MESH)

    def slot(ref, index, size=16):
        return ref.at[pl.ds(pl.multiple_of(index * size, size), size)]

    sent = []

    def push(src, dst, s, device):
        copy = pltpu.make_async_remote_copy(
            src_ref=src, dst_ref=dst, send_sem=send.at[s], recv_sem=recv.at[s],
            device_id=device, device_id_type=MESH,
        )
        copy.start()

    def arrived(ref, s, count, size):
        view = ref.at[pl.ds(0, count * size)]
        pltpu.make_async_copy(view, view, recv.at[s]).wait()
        sent.append((view, s))

    def halves(ref):
        whole = ref[...].astype(F32)
        return jnp.concatenate([whole[:, :half], whole[:, half:]], axis=0)

    loads[0].wait()
    slot(qb, z)[...] = halves(q_in).astype(BF16)
    loads[1].wait()
    slot(pb, y)[...] = halves(p_in).astype(BF16)
    pl.semaphore_wait(barrier, len(everyone))

    push(slot(qb, z), slot(qb, gz + z), SWAP_Q, x_peer)
    push(slot(pb, y), slot(pb, gy + y), SWAP_P, x_peer)
    for t in range(max(gy, gz) - 1):
        if t < gz - 1:
            push(slot(qb, z), slot(qb, z), OWN_Q, z_peers[t][1])
        if t < gy - 1:
            push(slot(pb, y), slot(pb, y), OWN_P, y_peers[t][1])

    loads[2].wait()
    loads[3].wait()
    spot = lax.broadcasted_iota(jnp.int32, (1, 1, 2 * nz), 2) % rows
    tag = jnp.zeros((1, 1, 2 * nz), jnp.int32)
    for i in range(rows):
        tag = jnp.where(spot == i, partner_ref[i], tag)
    tags[pl.ds(z, 1)] = tag.astype(F32)
    push(tags.at[pl.ds(z, 1)], tags.at[pl.ds(gz + z, 1)], SWAP_T, x_peer)

    arrived(qb, SWAP_Q, 1, 16)
    for _, device in z_peers[:3]:
        push(slot(qb, gz + z), slot(qb, gz + z), FAR_Q, device)
    arrived(pb, SWAP_P, 1, 16)
    for _, device in y_peers[:3]:
        push(slot(pb, gy + y), slot(pb, gy + y), FAR_P, device)
    for t in range(3, max(gy, gz) - 1):
        if t < gz - 1:
            push(slot(qb, gz + z), slot(qb, gz + z), FAR_Q, z_peers[t][1])
        if t < gy - 1:
            push(slot(pb, gy + y), slot(pb, gy + y), FAR_P, y_peers[t][1])
    arrived(tags, SWAP_T, 1, 1)
    for _, device in z_peers:
        push(tags.at[pl.ds(z, 1)], tags.at[pl.ds(z, 1)], OWN_T, device)
        push(tags.at[pl.ds(gz + z, 1)], tags.at[pl.ds(gz + z, 1)], FAR_T, device)

    def unpack(ref, out, r, n):
        whole = ref[r * n * 16:(r + 1) * n * 16, :half].astype(F32).reshape(n, 2, 8, half)
        whole = jnp.concatenate([whole[:, 0], whole[:, 1]], axis=2).reshape(n * 8, feats)
        out[r * n * 8:(r + 1) * n * 8, :] = whole.astype(BF16)
        square = whole * whole
        width = min(128, feats)
        return sum(square[:, c:c + width] for c in range(0, feats, width))

    arrived(qb, OWN_Q, gz - 1, 16)
    q_near = unpack(qb, qn, 0, gz)
    arrived(pb, OWN_P, gy - 1, 16)
    p_near = unpack(pb, pn, 0, gy)
    nh = nz // 2

    def fold(value):
        return jnp.concatenate([value[:nh], value[nh:]], axis=1)

    first[...] = fold(dot(qn[0:nz, :], pn[0:ny, :], NT))
    for device in left_peers:
        push(first, slot(first_left, core, nh), LEFT_E, device)
    for device in right_peers:
        push(first, slot(first_right, core, nh), RIGHT_E, device)
    push(first, first_core, CORE_E, core_peer)
    arrived(qb, FAR_Q, gz - 1, 16)
    q_far = unpack(qb, qn, 1, gz)
    part[0:nh, :] = fold(dot(qn[nz:, :], pn[0:ny, :], NT))
    tile = lax.broadcasted_iota(jnp.int32, (8, 2 * ny), 0)
    q_sum = jnp.sum(jnp.concatenate([q_near, q_far], axis=0).T, axis=0, keepdims=True)
    arrived(pb, FAR_P, gy - 1, 16)
    p_far = unpack(pb, pn, 1, gy)

    beyond = dot(qn[...], pn[ny:, :], NT)
    part[2 * nh:3 * nh, :] = fold(beyond[:nz])
    p_sum = jnp.sum(jnp.concatenate([p_near, p_far], axis=0).T, axis=0, keepdims=True)
    part[3 * nh:3 * nh + 8, :] = jnp.where(tile == 0, q_sum, p_sum)
    for device in left_peers:
        push(part.at[pl.ds(2 * nh, nh + 8)], slot(part_left, core, nh + 8), LEFT, device)
    for device in right_peers:
        push(part.at[pl.ds(2 * nh, nh)], slot(part_right, core, nh), RIGHT, device)
    part[nh:2 * nh, :] = fold(beyond[nz:])
    push(part, part_core, CORE, core_peer)
    arrived(tags, OWN_T, gz - 1, 1)
    arrived(tags, FAR_T, gz - 1, 1)
    seat = lax.broadcasted_iota(jnp.int32, (2 * gz, 1, 2 * nz), 2) // rows
    taken = seat == lax.broadcasted_iota(jnp.int32, (2 * gz, 1, 2 * nz), 0)
    partner = column(jnp.sum(jnp.where(taken, tags[...], 0.0), axis=0))
    lane = lax.broadcasted_iota(jnp.int32, (1, 2 * ny), 1)
    columns = (((x + lane // ny) % 2 * gy + lane // rows % gy) * gz + z) * rows + lane % rows
    hit = partner == columns.astype(F32)
    arrived(first_core, CORE_E, 1, nh)
    arrived(first_left, LEFT_E, 2, nh)
    arrived(first_right, RIGHT_E, 2, nh)
    arrived(part_core, CORE, 1, 3 * nh + 8)
    near = (first[...] + first_core[...]) + (first_left[0:nh, :] + first_left[nh:, :])
    right_near = first_right[0:nh, :] + first_right[nh:, :]
    total = part[...] + part_core[...]
    arrived(part_left, LEFT, 2, nh + 8)
    left = total[2 * nh:] + (part_left[0:nh + 8, :] + part_left[nh + 8:, :])
    arrived(part_right, RIGHT, 2, nh)
    right = part_right[0:nh, :] + part_right[nh:, :]
    lower = lane < ny

    def beside(a, b):
        return jnp.concatenate(
            [jnp.where(lower, a, pltpu.roll(b, ny, 1)), jnp.where(lower, pltpu.roll(a, ny, 1), b)], axis=0
        )

    product = jnp.concatenate(
        [beside(near, left[:nh]), beside(total[:nh] + right, total[nh:2 * nh] + right_near)], axis=0
    )
    sums = left[nh:]

    scale = scale_ref[0]
    q_inv = column(lax.rsqrt(sums[0:1] + 1e-6))
    p_inv = lax.rsqrt(sums[1:2] + 1e-6)
    scores = (product * q_inv) * p_inv * scale
    across = scores.T

    def added(value, n):
        return jnp.sum(value[:n], axis=0, keepdims=True) + jnp.sum(value[n:], axis=0, keepdims=True)

    def both(row, n):
        return jnp.sum(row[:, :n]) + jnp.sum(row[:, n:])

    row_max = jnp.max(across, axis=0, keepdims=True)
    row_exp = jnp.exp(across - row_max)
    row_sum = added(row_exp, ny)
    col_max = jnp.max(scores, axis=0, keepdims=True)
    col_exp = jnp.exp(scores - col_max)
    col_sum = added(col_exp, nz)
    held = jnp.where(hit, scores, 0.0)
    near, far = (jnp.sum(held[r:r + nz], axis=0, keepdims=True) for r in (0, nz))
    hits = (jnp.sum(near[:, :ny]) + jnp.sum(far[:, ny:])) + (jnp.sum(near[:, ny:]) + jnp.sum(far[:, :ny]))
    for i, value in enumerate((row_max, row_sum, jnp.full((1, 2 * nz), hits))):
        row_stat[i] = value
    for i, value in enumerate((col_max, col_sum)):
        col_stat[i] = value
    for t in range(max(gy, gz) - 1):
        if t < gz - 1:
            push(row_stat, slot(row_stats, z, 3), ROWS, z_peers[t][1])
        if t < gy - 1:
            push(col_stat, slot(col_stats, y, 2), COLS, y_peers[t][1])
    slot(row_stats, z, 3)[...] = row_stat[...]
    slot(col_stats, y, 2)[...] = col_stat[...]

    def units(raw, inv, less, n):
        inv = inv[:, :1]
        unit = raw[...].astype(F32) * inv
        raw[...] = unit.astype(BF16)
        less[...] = unit[:n] * inv[:n]
        return scale * inv[:n]

    q_scale = units(qn, q_inv, q_less, nz)
    p_scale = units(pn, column(p_inv), p_less, ny)
    row_exp = row_exp.T * (0.5 / pairs)
    col_exp = col_exp * (0.5 / pairs)
    hit = jnp.where(hit, 1.0 / pairs, 0.0)

    def lse(ref, n):
        stats = ref[...].reshape(n, -1, 1, ref.shape[2])
        most = jnp.max(stats[:, 0], axis=0)
        summed = jnp.sum(stats[:, 1] * jnp.exp(stats[:, 0] - most), axis=0)
        return most + jnp.log(summed), stats

    arrived(row_stats, ROWS, gz - 1, 3)
    row_lse, stats = lse(row_stats, gz)
    row_part = column(jnp.exp(row_max - row_lse))
    arrived(col_stats, COLS, gy - 1, 2)
    col_lse, _ = lse(col_stats, gy)

    weights = row_exp * row_part + col_exp * jnp.exp(col_max - col_lse) - hit
    weights = weights.astype(BF16).astype(F32)
    turned = weights.T[:ny]
    weights = weights[:nz]

    def share(weight, score, other, scaled, less):
        n = weight.shape[0]
        d = dot(weight.astype(BF16), other, NN)
        along = jnp.sum(weight * score, axis=1, keepdims=True)
        d = (d * scaled - less * along).reshape(n // 8, 8, feats)
        return jnp.concatenate([d[:, :, :half], d[:, :, half:]], axis=1).reshape(n * 2, half)

    positives = jnp.sum(stats[:, 2, 0, 0:1])
    loss_part[0] = jnp.full((1, 128), 0.5 * both(col_lse, ny))
    loss_part[1] = jnp.full((1, 128), 0.5 * both(row_lse, nz) - positives)
    for _, device in z_peers:
        push(loss_part.at[pl.ds(0, 1)], loss_z.at[pl.ds(z, 1)], LOSS_Z, device)
    for _, device in y_peers:
        push(loss_part.at[pl.ds(1, 1)], loss_y.at[pl.ds(y, 1)], LOSS_Y, device)

    gq[...] = share(weights, scores[:nz], pn[...], q_scale, q_less[...]).astype(BF16)
    for i, device in z_peers[:3]:
        push(slot(gq, i), slot(rq, z), GRAD_Q, device)
    gp[...] = share(turned, across[:ny], qn[...], p_scale, p_less[...]).astype(BF16)
    for i, device in y_peers[:3]:
        push(slot(gp, i), slot(rp, y), GRAD_P, device)
    for t in range(3, max(gy, gz) - 1):
        if t < gz - 1:
            push(slot(gq, z_peers[t][0]), slot(rq, z), GRAD_Q, z_peers[t][1])
        if t < gy - 1:
            push(slot(gp, y_peers[t][0]), slot(rp, y), GRAD_P, y_peers[t][1])
    keeps = [
        pltpu.make_async_copy(source, target, load.at[i])
        for i, (source, target) in enumerate((
            (slot(gq, z), slot(rq, z)),
            (slot(gp, y), slot(rp, y)),
            (loss_part.at[pl.ds(0, 1)], loss_z.at[pl.ds(z, 1)]),
            (loss_part.at[pl.ds(1, 1)], loss_y.at[pl.ds(y, 1)]),
        ))
    ]
    for copy in keeps:
        copy.start()
    for copy in keeps:
        copy.wait()
    arrived(rq, GRAD_Q, gz - 1, 16)
    arrived(rp, GRAD_P, gy - 1, 16)
    arrived(loss_z, LOSS_Z, gz - 1, 1)
    arrived(loss_y, LOSS_Y, gy - 1, 1)
    for view, s in sent:
        pltpu.make_async_copy(view, view, send.at[s]).wait()


def finish(pairs, rq, rp, loss_z, loss_y, loss_ref, gq_ref, gp_ref):
    half = gq_ref.shape[1] // 2

    for ref, out_ref in ((rq, gq_ref), (rp, gp_ref)):
        whole = jnp.sum(ref[...].astype(F32).reshape(-1, 16, half), axis=0)
        out_ref[...] = jnp.concatenate([whole[:8], whole[8:]], axis=1).astype(BF16)
    parts = jnp.sum(loss_z[...], axis=0) + jnp.sum(loss_y[...], axis=0)
    loss_ref[0] = jnp.sum(parts[:, 0:1]) / pairs


def build(mesh, grid):
    _, gy, gz = grid

    def shards(queries, paraphrases, partner, logit_scale):
        rows, feats = queries.shape
        half = feats // 2
        nz, ny = gz * rows, gy * rows
        vmem, smem = pl.BlockSpec(memory_space=pltpu.VMEM), pl.BlockSpec(memory_space=pltpu.SMEM)
        anywhere = pl.BlockSpec(memory_space=pl.ANY)
        block = pltpu.VMEM((nz + nz // 2 + 8, 2 * ny), F32)
        shares = pl.pallas_call(
            functools.partial(kernel, grid),
            out_shape=(
                jax.ShapeDtypeStruct((gz * 16, half), BF16),
                jax.ShapeDtypeStruct((gy * 16, half), BF16),
                jax.ShapeDtypeStruct((gz, 1, 128), F32),
                jax.ShapeDtypeStruct((gy, 1, 128), F32),
            ),
            in_specs=[anywhere] * 4,
            out_specs=(anywhere,) * 4,
            scratch_shapes=[
                pltpu.SMEM((1,), F32),
                pltpu.SMEM((rows,), jnp.int32),
                pltpu.VMEM((rows, feats), BF16),
                pltpu.VMEM((rows, feats), BF16),
                pltpu.VMEM((gz * 32, half), BF16),
                pltpu.VMEM((gy * 32, half), BF16),
                pltpu.VMEM((2 * nz, feats), BF16),
                pltpu.VMEM((2 * ny, feats), BF16),
                block,
                block,
                pltpu.VMEM((nz + 16, 2 * ny), F32),
                pltpu.VMEM((nz, 2 * ny), F32),
                pltpu.VMEM((nz // 2, 2 * ny), F32),
                pltpu.VMEM((nz // 2, 2 * ny), F32),
                pltpu.VMEM((nz, 2 * ny), F32),
                pltpu.VMEM((nz, 2 * ny), F32),
                pltpu.VMEM((3, 1, 2 * nz), F32),
                pltpu.VMEM((gz * 3, 1, 2 * nz), F32),
                pltpu.VMEM((2, 1, 2 * ny), F32),
                pltpu.VMEM((gy * 2, 1, 2 * ny), F32),
                pltpu.VMEM((gz * 16, half), BF16),
                pltpu.VMEM((gy * 16, half), BF16),
                pltpu.VMEM((2 * gz, 1, 2 * nz), F32),
                pltpu.VMEM((nz, feats), F32),
                pltpu.VMEM((ny, feats), F32),
                pltpu.VMEM((2, 1, 128), F32),
                pltpu.SemaphoreType.DMA((4,)),
                pltpu.SemaphoreType.DMA((21,)),
                pltpu.SemaphoreType.DMA((21,)),
            ],
            compiler_params=pltpu.CompilerParams(
                collective_id=0, has_side_effects=True, vmem_limit_bytes=32 * 1024 * 1024
            ),
        )(logit_scale.reshape(1), pltpu.with_memory_space_constraint(partner, pltpu.HBM), pltpu.with_memory_space_constraint(queries, pltpu.HBM), pltpu.with_memory_space_constraint(paraphrases, pltpu.HBM))
        loss, grad_q, grad_p = pl.pallas_call(
            functools.partial(finish, 2 * gy * nz),
            out_shape=(
                jax.ShapeDtypeStruct((1,), F32),
                jax.ShapeDtypeStruct((rows, feats), BF16),
                jax.ShapeDtypeStruct((rows, feats), BF16),
            ),
            in_specs=[vmem] * 4,
            out_specs=(smem, vmem, vmem),
            compiler_params=pltpu.CompilerParams(vmem_limit_bytes=4 * 1024 * 1024),
        )(*shares)
        return loss[0], grad_q, grad_p

    if mesh is None:
        return shards
    return jax.shard_map(
        shards,
        mesh=mesh,
        in_specs=(P("batch", "mp"), P("batch", "mp"), P("batch"), P()),
        out_specs=(P(), P("batch", "mp"), P("batch", "mp")),
        check_vma=False,
    )


def solution(mesh):
    return build(mesh, GRID)
```

time: 42.1 us -> 39.6 us (0.941)
  Pallas kernels: 40.6 us -> 38.1 us
    pallas_call x1, Pallas kernels: 38.9 us -> 37.5 us  [shards(): pl.pallas_call(functools.partial(kernel, grid), out_shape=(jax.ShapeDtype...]
    pallas_call x1, Pallas kernels: 1.65 us -> 0.65 us  [shards(): pl.pallas_call(functools.partial(finish, 2 * gy * nz), out_shape=(jax.Sha...]
where the time goes in v3:
time: 39.6 us; the launch traced here: 39.4 us
  Pallas kernels  38.1 us (96%)
  between operations  1.29 us (3%)
    pallas_call x1, Pallas kernels, shards(): pl.pallas_call(functools.partial(kernel, grid), out_shape=(jax.ShapeDtype...  37.5 us

profile of v3, /device:TPU:1, one launch (start us, length us, event | category | flops | bytes accessed | tf_op | source)
XLA Modules:
  0.0 39.4 jit_solution(5237522600696137764)
XLA Ops:
  1.3 37.5 %shard_map.67 = (bf16[128,512]{1,0:T(8,128)(2,1)S(1)}, bf16[128,512]{1,0:T(8,128)(2,1)S(1)}, f32[8,1,128]{2,1,0:T(1,128)S(1)}, f32[8,1,128]{2,1,0:T(1,128)S(1)}) custom-call(f32[1]{0:T(128)} %bitcast.2.scale_any, s32[8]{0:T(128)} %partner_any.1, bf16[8,1024]{1,0:T(8,128)(2,1)} %q_any.1, bf16[8,1024]{1,0:T(8,128)(2,1)} %p_any.1), custom_call_target="tpu_custom_call" | custom-call | tf_op jit(solution)/shard_map/pallas_call | solution.py:330
  38.7 0.7 %shard_map.68 = (f32[1]{0:T(128)}, bf16[8,1024]{1,0:T(8,128)(2,1)}, bf16[8,1024]{1,0:T(8,128)(2,1)}) custom-call(bf16[128,512]{1,0:T(8,128)(2,1)S(1)} %get-tuple-element.10.rq, bf16[128,512]{1,0:T(8,128)(2,1)S(1)} %get-tuple-element.11.rp, f32[8,1,128]{2,1,0:T(1,128)S(1)} %get-tuple-element.12.loss_z, f32[8,1,128]{2,1,0:T(1,128)S(1)} %get-tuple-element.13.loss_y), custom_call_target="tpu_custom_call" | custom-call | tf_op jit(solution)/shard_map/pallas_call | solution.py:375

commit v4 on v3

--- a/solution.py
+++ b/solution.py
@@ -52,6 +52,10 @@
     left_peers = [{"mp": other + c} for c in range(2)]
     right_peers = [{"batch": x_peer["batch"], "mp": other + c} for c in range(2)]
 
+    barrier = pltpu.get_barrier_semaphore()
+    everyone = [x_peer] + [d for pair in zip(z_peers, y_peers) for _, d in pair] + [*left_peers, *right_peers, core_peer]
+    for d in everyone:
+        pl.semaphore_signal(barrier, inc=1, device_id=d, device_id_type=MESH)
     loads = [
         pltpu.make_async_copy(source, target, load.at[i])
         for i, (source, target) in enumerate(
@@ -60,10 +64,6 @@
     ]
     for copy in loads:
         copy.start()
-    barrier = pltpu.get_barrier_semaphore()
-    everyone = [x_peer] + [d for pair in zip(z_peers, y_peers) for _, d in pair] + [*left_peers, *right_peers, core_peer]
-    for d in everyone:
-        pl.semaphore_signal(barrier, inc=1, device_id=d, device_id_type=MESH)
 
     def slot(ref, index, size=16):
         return ref.at[pl.ds(pl.multiple_of(index * size, size), size)]
@@ -81,6 +81,11 @@
         view = ref.at[pl.ds(0, count * size)]
         pltpu.make_async_copy(view, view, recv.at[s]).wait()
         sent.append((view, s))
+
+    def departed():
+        for view, s in sent:
+            pltpu.make_async_copy(view, view, send.at[s]).wait()
+        sent.clear()
 
     def halves(ref):
         whole = ref[...].astype(F32)
@@ -142,29 +147,30 @@
     def fold(value):
         return jnp.concatenate([value[:nh], value[nh:]], axis=1)
 
-    first[...] = fold(dot(qn[0:nz, :], pn[0:ny, :], NT))
+    def sums(q_square, p_square):
+        row = jnp.sum(jnp.concatenate([q_square, p_square], axis=0).T, axis=0, keepdims=True)
+        return jnp.broadcast_to(row, (8, 2 * ny))
+
+    first[0:nh, :] = fold(dot(qn[0:nz, :], pn[0:ny, :], NT))
+    first[nh:nh + 8, :] = sums(q_near, p_near)
     for device in left_peers:
-        push(first, slot(first_left, core, nh), LEFT_E, device)
+        push(first, slot(first_left, core, nh + 8), LEFT_E, device)
     for device in right_peers:
-        push(first, slot(first_right, core, nh), RIGHT_E, device)
+        push(first, slot(first_right, core, nh + 8), RIGHT_E, device)
     push(first, first_core, CORE_E, core_peer)
+
+    arrived(pb, FAR_P, gy - 1, 16)
+    p_far = unpack(pb, pn, 1, gy)
+    part[nz:nz + nh, :] = fold(dot(qn[0:nz, :], pn[ny:, :], NT))
+    for device in left_peers:
+        push(part.at[pl.ds(nz, nh)], slot(part_left, core, nh), LEFT, device)
+    for device in right_peers:
+        push(part.at[pl.ds(nz, nh)], slot(part_right, core, nh), RIGHT, device)
     arrived(qb, FAR_Q, gz - 1, 16)
     q_far = unpack(qb, qn, 1, gz)
-    part[0:nh, :] = fold(dot(qn[nz:, :], pn[0:ny, :], NT))
-    tile = lax.broadcasted_iota(jnp.int32, (8, 2 * ny), 0)
-    q_sum = jnp.sum(jnp.concatenate([q_near, q_far], axis=0).T, axis=0, keepdims=True)
-    arrived(pb, FAR_P, gy - 1, 16)
-    p_far = unpack(pb, pn, 1, gy)
-
-    beyond = dot(qn[...], pn[ny:, :], NT)
-    part[2 * nh:3 * nh, :] = fold(beyond[:nz])
-    p_sum = jnp.sum(jnp.concatenate([p_near, p_far], axis=0).T, axis=0, keepdims=True)
-    part[3 * nh:3 * nh + 8, :] = jnp.where(tile == 0, q_sum, p_sum)
-    for device in left_peers:
-        push(part.at[pl.ds(2 * nh, nh + 8)], slot(part_left, core, nh + 8), LEFT, device)
-    for device in right_peers:
-        push(part.at[pl.ds(2 * nh, nh)], slot(part_right, core, nh), RIGHT, device)
-    part[nh:2 * nh, :] = fold(beyond[nz:])
+
+    part[0:nz, :] = dot(qn[nz:, :], pn[...], NT)
+    part[nz + nh:nz + nh + 8, :] = sums(q_far, p_far)
     push(part, part_core, CORE, core_peer)
     arrived(tags, OWN_T, gz - 1, 1)
     arrived(tags, FAR_T, gz - 1, 1)
@@ -174,15 +180,15 @@
     lane = lax.broadcasted_iota(jnp.int32, (1, 2 * ny), 1)
     columns = (((x + lane // ny) % 2 * gy + lane // rows % gy) * gz + z) * rows + lane % rows
     hit = partner == columns.astype(F32)
-    arrived(first_core, CORE_E, 1, nh)
-    arrived(first_left, LEFT_E, 2, nh)
-    arrived(first_right, RIGHT_E, 2, nh)
+    arrived(first_core, CORE_E, 1, nh + 8)
+    arrived(first_left, LEFT_E, 2, nh + 8)
+    arrived(first_right, RIGHT_E, 2, nh + 8)
+    near = (first[...] + first_core[...]) + (first_left[0:nh + 8, :] + first_left[nh + 8:, :])
+    right_near = first_right[0:nh + 8, :] + first_right[nh + 8:, :]
     arrived(part_core, CORE, 1, 3 * nh + 8)
-    near = (first[...] + first_core[...]) + (first_left[0:nh, :] + first_left[nh:, :])
-    right_near = first_right[0:nh, :] + first_right[nh:, :]
     total = part[...] + part_core[...]
-    arrived(part_left, LEFT, 2, nh + 8)
-    left = total[2 * nh:] + (part_left[0:nh + 8, :] + part_left[nh + 8:, :])
+    arrived(part_left, LEFT, 2, nh)
+    left = total[nz:nz + nh] + (part_left[0:nh, :] + part_left[nh:, :])
     arrived(part_right, RIGHT, 2, nh)
     right = part_right[0:nh, :] + part_right[nh:, :]
     lower = lane < ny
@@ -192,14 +198,12 @@
             [jnp.where(lower, a, pltpu.roll(b, ny, 1)), jnp.where(lower, pltpu.roll(a, ny, 1), b)], axis=0
         )
 
-    product = jnp.concatenate(
-        [beside(near, left[:nh]), beside(total[:nh] + right, total[nh:2 * nh] + right_near)], axis=0
-    )
-    sums = left[nh:]
+    product = jnp.concatenate([beside(near[:nh], left), total[:nz] + beside(right, right_near[:nh])], axis=0)
+    squares = beside(near[nh:nh + 8], total[nz + nh:] + right_near[nh:])
 
     scale = scale_ref[0]
-    q_inv = column(lax.rsqrt(sums[0:1] + 1e-6))
-    p_inv = lax.rsqrt(sums[1:2] + 1e-6)
+    q_inv = column(lax.rsqrt(squares[0:1] + 1e-6))
+    p_inv = lax.rsqrt(squares[8:9] + 1e-6)
     scores = (product * q_inv) * p_inv * scale
     across = scores.T
 
@@ -299,12 +303,12 @@
         copy.start()
     for copy in keeps:
         copy.wait()
+    departed()
     arrived(rq, GRAD_Q, gz - 1, 16)
     arrived(rp, GRAD_P, gy - 1, 16)
     arrived(loss_z, LOSS_Z, gz - 1, 1)
     arrived(loss_y, LOSS_Y, gy - 1, 1)
-    for view, s in sent:
-        pltpu.make_async_copy(view, view, send.at[s]).wait()
+    departed()
 
 
 def finish(pairs, rq, rp, loss_z, loss_y, loss_ref, gq_ref, gp_ref):
@@ -348,12 +352,12 @@
                 pltpu.VMEM((2 * ny, feats), BF16),
                 block,
                 block,
-                pltpu.VMEM((nz + 16, 2 * ny), F32),
-                pltpu.VMEM((nz, 2 * ny), F32),
-                pltpu.VMEM((nz // 2, 2 * ny), F32),
-                pltpu.VMEM((nz // 2, 2 * ny), F32),
                 pltpu.VMEM((nz, 2 * ny), F32),
                 pltpu.VMEM((nz, 2 * ny), F32),
+                pltpu.VMEM((nz // 2 + 8, 2 * ny), F32),
+                pltpu.VMEM((nz // 2 + 8, 2 * ny), F32),
+                pltpu.VMEM((nz + 16, 2 * ny), F32),
+                pltpu.VMEM((nz + 16, 2 * ny), F32),
                 pltpu.VMEM((3, 1, 2 * nz), F32),
                 pltpu.VMEM((gz * 3, 1, 2 * nz), F32),
                 pltpu.VMEM((2, 1, 2 * ny), F32),

time: 39.6 us -> 39.6 us (level)
  no operation moved by 1% of the time
where the time goes in v4:
time: 39.6 us; the launch traced here: 39.4 us
  Pallas kernels  38.1 us (96%)
  between operations  1.29 us (3%)
    pallas_call x1, Pallas kernels, shards(): pl.pallas_call(functools.partial(kernel, grid), out_shape=(jax.ShapeDtype...  37.4 us

profile of v4, /device:TPU:1, one launch (start us, length us, event | category | flops | bytes accessed | tf_op | source)
XLA Modules:
  0.0 39.4 jit_solution(16042245023370584794)
XLA Ops:
  1.3 37.4 %shard_map.67 = (bf16[128,512]{1,0:T(8,128)(2,1)S(1)}, bf16[128,512]{1,0:T(8,128)(2,1)S(1)}, f32[8,1,128]{2,1,0:T(1,128)S(1)}, f32[8,1,128]{2,1,0:T(1,128)S(1)}) custom-call(f32[1]{0:T(128)} %bitcast.2.scale_any, s32[8]{0:T(128)} %partner_any.1, bf16[8,1024]{1,0:T(8,128)(2,1)} %q_any.1, bf16[8,1024]{1,0:T(8,128)(2,1)} %p_any.1), custom_call_target="tpu_custom_call" | custom-call | tf_op jit(solution)/shard_map/pallas_call | solution.py:334
  38.7 0.7 %shard_map.68 = (f32[1]{0:T(128)}, bf16[8,1024]{1,0:T(8,128)(2,1)}, bf16[8,1024]{1,0:T(8,128)(2,1)}) custom-call(bf16[128,512]{1,0:T(8,128)(2,1)S(1)} %get-tuple-element.10.rq, bf16[128,512]{1,0:T(8,128)(2,1)S(1)} %get-tuple-element.11.rp, f32[8,1,128]{2,1,0:T(1,128)S(1)} %get-tuple-element.12.loss_z, f32[8,1,128]{2,1,0:T(1,128)S(1)} %get-tuple-element.13.loss_y), custom_call_target="tpu_custom_call" | custom-call | tf_op jit(solution)/shard_map/pallas_call | solution.py:379

commit v5 on v4

--- a/solution.py
+++ b/solution.py
@@ -30,8 +30,8 @@
     return sorted(range(1, n), key=lambda t: -min(t, n - t))
 
 
-def kernel(grid, scale_any, partner_any, q_any, p_any, rq, rp, loss_z, loss_y,
-           scale_ref, partner_ref, q_in, p_in, qb, pb, qn, pn, part, part_core, part_left, part_right,
+def kernel(grid, scale_ref, partner_any, q_any, p_any, rq, rp, loss_z, loss_y,
+           partner_ref, q_in, p_in, qb, pb, qn, pn, part, part_core, part_left, part_right,
            first, first_core, first_left, first_right,
            row_stat, row_stats, col_stat, col_stats, gq, gp, tags, q_less, p_less, loss_part, load, send, recv):
     _, gy, gz = grid
@@ -59,7 +59,7 @@
     loads = [
         pltpu.make_async_copy(source, target, load.at[i])
         for i, (source, target) in enumerate(
-            ((q_any, q_in), (p_any, p_in), (partner_any, partner_ref), (scale_any, scale_ref))
+            ((q_any, q_in), (p_any, p_in), (partner_any, partner_ref))
         )
     ]
     for copy in loads:
@@ -106,7 +106,6 @@
             push(slot(pb, y), slot(pb, y), OWN_P, y_peers[t][1])
 
     loads[2].wait()
-    loads[3].wait()
     spot = lax.broadcasted_iota(jnp.int32, (1, 1, 2 * nz), 2) % rows
     tag = jnp.zeros((1, 1, 2 * nz), jnp.int32)
     for i in range(rows):
@@ -201,7 +200,7 @@
     product = jnp.concatenate([beside(near[:nh], left), total[:nz] + beside(right, right_near[:nh])], axis=0)
     squares = beside(near[nh:nh + 8], total[nz + nh:] + right_near[nh:])
 
-    scale = scale_ref[0]
+    scale = scale_ref[...]
     q_inv = column(lax.rsqrt(squares[0:1] + 1e-6))
     p_inv = lax.rsqrt(squares[8:9] + 1e-6)
     scores = (product * q_inv) * p_inv * scale
@@ -339,10 +338,7 @@
                 jax.ShapeDtypeStruct((gz, 1, 128), F32),
                 jax.ShapeDtypeStruct((gy, 1, 128), F32),
             ),
-            in_specs=[anywhere] * 4,
-            out_specs=(anywhere,) * 4,
-            scratch_shapes=[
-                pltpu.SMEM((1,), F32),
+            grid_spec=pltpu.PrefetchScalarGridSpec(num_scalar_prefetch=1, grid=(), in_specs=[anywhere] * 3, out_specs=(anywhere,) * 4, scratch_shapes=[
                 pltpu.SMEM((rows,), jnp.int32),
                 pltpu.VMEM((rows, feats), BF16),
                 pltpu.VMEM((rows, feats), BF16),
@@ -371,11 +367,11 @@
                 pltpu.SemaphoreType.DMA((4,)),
                 pltpu.SemaphoreType.DMA((21,)),
                 pltpu.SemaphoreType.DMA((21,)),
-            ],
+            ]),
             compiler_params=pltpu.CompilerParams(
                 collective_id=0, has_side_effects=True, vmem_limit_bytes=32 * 1024 * 1024
             ),
-        )(logit_scale.reshape(1), pltpu.with_memory_space_constraint(partner, pltpu.HBM), pltpu.with_memory_space_constraint(queries, pltpu.HBM), pltpu.with_memory_space_constraint(paraphrases, pltpu.HBM))
+        )(logit_scale, pltpu.with_memory_space_constraint(partner, pltpu.HBM), pltpu.with_memory_space_constraint(queries, pltpu.HBM), pltpu.with_memory_space_constraint(paraphrases, pltpu.HBM))
         loss, grad_q, grad_p = pl.pallas_call(
             functools.partial(finish, 2 * gy * nz),
             out_shape=(

time: 39.6 us -> 39.6 us (level)
  no operation moved by 1% of the time
where the time goes in v5:
time: 39.6 us; the launch traced here: 39.4 us
  Pallas kernels  38.1 us (96%)
  between operations  1.29 us (3%)
    pallas_call x1, Pallas kernels, shards(): pl.pallas_call(functools.partial(kernel, grid), out_shape=(jax.ShapeDtype...  37.4 us

profile of v5, /device:TPU:1, one launch (start us, length us, event | category | flops | bytes accessed | tf_op | source)
XLA Modules:
  0.0 39.4 jit_solution(1488585138724244555)
XLA Ops:
  1.3 37.4 %shard_map.67 = (bf16[128,512]{1,0:T(8,128)(2,1)S(1)}, bf16[128,512]{1,0:T(8,128)(2,1)S(1)}, f32[8,1,128]{2,1,0:T(1,128)S(1)}, f32[8,1,128]{2,1,0:T(1,128)S(1)}) custom-call(f32[]{:T(128)S(6)} %copy.7.scale_ref, s32[8]{0:T(128)} %partner_any.1, bf16[8,1024]{1,0:T(8,128)(2,1)} %q_any.1, bf16[8,1024]{1,0:T(8,128)(2,1)} %p_any.1), custom_call_target="tpu_custom_call" | custom-call | tf_op jit(solution)/shard_map/pallas_call | solution.py:333
  38.7 0.7 %shard_map.68 = (f32[1]{0:T(128)}, bf16[8,1024]{1,0:T(8,128)(2,1)}, bf16[8,1024]{1,0:T(8,128)(2,1)}) custom-call(bf16[128,512]{1,0:T(8,128)(2,1)S(1)} %get-tuple-element.10.rq, bf16[128,512]{1,0:T(8,128)(2,1)S(1)} %get-tuple-element.11.rp, f32[8,1,128]{2,1,0:T(1,128)S(1)} %get-tuple-element.12.loss_z, f32[8,1,128]{2,1,0:T(1,128)S(1)} %get-tuple-element.13.loss_y), custom_call_target="tpu_custom_call" | custom-call | tf_op jit(solution)/shard_map/pallas_call | solution.py:375
